TPU v7x, 128 devices: a whole 4x4x4 slice. The times are simulated.
128 devices in a mesh: dp: 32 (over z, y, core), sp: 4 (over x).
Axes of the slice: x: 4, y: 4, z: 4, core: 2. Of those that a mesh axis runs over, the one named last changes fastest.
Arguments:
- tokens: bfloat16 [32768, 8192], P(('dp', 'sp')), may hold values from -24 to 24
- value_projection_matrix: bfloat16 [8192, 512], P(('dp', 'sp')), may hold values from -0.0625 to 0.0625
- queries: bfloat16 [32768, 4096], P(('dp', 'sp')), may hold values from -80 to 80, as said below
- rotated_key_rows: bfloat16 [32768, 512], P(('dp', 'sp')), may hold values from -80 to 80, as said below
- output_cotangent: bfloat16 [32768, 4096], P(('dp', 'sp')), may hold values from -6 to 6
- block_dest: int32 [4096], P(('dp', 'sp')), may hold values from 0 to 4095, as said below
- doc_ids: int32 [32, 1024], P('dp'), may hold values from 0 to 1, as said below
Outputs:
- query_gradient: bfloat16 [32768, 4096], P(('dp', 'sp'))
- key_gradient: bfloat16 [32768, 512], P(('dp', 'sp'))
- weight_grad: float32 [8192, 512], P(('dp', 'sp'))
Inputs may be any that keep to these rules, and one draw needn't show every extreme that they name: block_dest is a permutation of the 4096 blocks; block b belongs to device b // 32 and lands in group-order block block_dest[b], held by device block_dest[b] // 32, which lies in the same sp index; every device receives exactly 32 blocks; at most 2 blocks pass from one device to one device; along dp, block k of a device of sp index j moves a number of places (cyclically) that depends only on j and k. `doc_ids`: in each group the ids start at 0 and never fall; equal ids form one document; a group holds one or two documents, and a second one begins between positions 256 and 768. `queries`: rows g * 1024 to (g + 1) * 1024 - 1 are the positions of group g in order. `rotated_key_rows`: rows g * 1024 to (g + 1) * 1024 - 1 are the positions of group g in order.
All inputs are finite; a program needn't handle non-finite values.
Results may differ from a plain program's by a relative error of at most 0.02.
Values may be sent and summed in bfloat16 or wider, within the bound.
A program may use at most 128 MiB of HBM per device.

v0:
```python
import math

import jax
import jax.numpy as jnp
from jax import lax
from jax.sharding import PartitionSpec as P

HEAD_SIZE = 128
QUERY_HEADS = 32
KEY_VALUE_HEADS = 4


def routing_plan(destination, block_count, sp_count, peer_most):
    dest_device = destination // block_count
    peer_index = dest_device // sp_count
    target = destination % block_count
    ordinal = jnp.arange(block_count, dtype=jnp.int32)
    same_peer = (peer_index[None, :] == peer_index[:, None]) & (ordinal[None, :] < ordinal[:, None])
    peer_rank = jnp.sum(same_peer.astype(jnp.int32), axis=1)
    return (peer_index * peer_most + peer_rank, target)


def pack_blocks(blocks, position, target, dp_count, peer_most):
    slot_total = dp_count * peer_most
    buffer = jnp.zeros((slot_total,) + blocks.shape[1:], blocks.dtype).at[position].set(blocks)
    labels = jnp.full((slot_total,), -1.0, jnp.float32).at[position].set(target.astype(jnp.float32))
    packed = buffer.reshape(dp_count, peer_most * blocks.shape[1], blocks.shape[2])
    return (packed, labels.reshape(dp_count, peer_most).astype(jnp.bfloat16))


def unpack_blocks(received, arrived, block_count, block_rows):
    flat = received.reshape(-1, block_rows, received.shape[-1])
    wanted = jnp.arange(block_count, dtype=jnp.int32)
    source_slot = jnp.argmax((arrived[None, :] == wanted[:, None]).astype(jnp.int32), axis=1)
    return flat[source_slot].reshape(block_count * block_rows, received.shape[-1])


def attend_local(head_queries, head_keys, head_values, head_grads, document):
    group_len = head_queries.shape[0]
    kv_heads = head_keys.shape[1] // HEAD_SIZE
    heads_per_group = QUERY_HEADS // KEY_VALUE_HEADS
    score_scale = 1.0 / math.sqrt(HEAD_SIZE)
    block_len = min(512, group_len)
    block_count = group_len // block_len
    query_blocks = head_queries.reshape(
        block_count, block_len, kv_heads, heads_per_group, HEAD_SIZE
    )
    grad_blocks = head_grads.reshape(block_count, block_len, kv_heads, heads_per_group, HEAD_SIZE)
    key_three = head_keys.reshape(group_len, kv_heads, HEAD_SIZE)
    value_three = head_values.reshape(group_len, kv_heads, HEAD_SIZE)
    positions = jnp.arange(group_len, dtype=jnp.int32)

    def query_block(totals, inputs):
        key_total, value_total = totals
        block_queries, block_grads, block_index = inputs
        query_pos = block_index * block_len + jnp.arange(block_len, dtype=jnp.int32)
        query_doc = lax.dynamic_slice_in_dim(document, block_index * block_len, block_len)
        allowed = (query_doc[:, None] == document[None, :]) & (
            positions[None, :] <= query_pos[:, None]
        )
        scores = (
            jnp.einsum(
                "qgrd,kgd->grqk", block_queries, key_three, preferred_element_type=jnp.float32
            )
            * score_scale
        )
        scores = jnp.where(allowed, scores, -1e30)
        row_max = jnp.max(scores, axis=-1, keepdims=True)
        weights_raw = jnp.exp(scores - row_max)
        probability = weights_raw / jnp.sum(weights_raw, axis=-1, keepdims=True)
        prob_low = probability.astype(jnp.bfloat16)
        attended = jnp.einsum(
            "grqk,kgd->qgrd", prob_low, value_three, preferred_element_type=jnp.float32
        )
        row_dot = jnp.sum(block_grads.astype(jnp.float32) * attended, axis=-1)
        dprob = jnp.einsum(
            "qgrd,kgd->grqk", block_grads, value_three, preferred_element_type=jnp.float32
        )
        dscore = probability * (dprob - jnp.transpose(row_dot, (1, 2, 0))[..., None])
        dscore_low = dscore.astype(jnp.bfloat16)
        query_part = jnp.einsum(
            "grqk,kgd->qgrd", dscore_low, key_three, preferred_element_type=jnp.float32
        )
        query_part = (query_part * score_scale).astype(jnp.bfloat16).reshape(block_len, -1)
        key_total = key_total + jnp.einsum(
            "grqk,qgrd->kgd", dscore_low, block_queries, preferred_element_type=jnp.float32
        )
        value_total = value_total + jnp.einsum(
            "grqk,qgrd->kgd", prob_low, block_grads, preferred_element_type=jnp.float32
        )
        return ((key_total, value_total), query_part)

    zeros_start = jnp.zeros((group_len, kv_heads, HEAD_SIZE), jnp.float32)
    totals, query_parts = lax.scan(
        query_block,
        (zeros_start, zeros_start),
        (query_blocks, grad_blocks, jnp.arange(block_count, dtype=jnp.int32)),
    )
    key_gradient = (totals[0] * score_scale).astype(jnp.bfloat16).reshape(group_len, -1)
    value_gradient = totals[1].astype(jnp.bfloat16).reshape(group_len, -1)
    return (query_parts.reshape(group_len, -1), key_gradient, value_gradient)


def per_device(
    tokens,
    value_projection_matrix,
    queries,
    rotated_key_rows,
    output_cotangent,
    block_dest,
    doc_ids,
):
    dp_count = lax.axis_size("dp")
    sp_count = lax.axis_size("sp")
    tok_count = tokens.shape[0]
    block_count = block_dest.shape[0]
    block_rows = tok_count // block_count
    peer_most = block_count // dp_count + 1
    weight_full = lax.all_gather(value_projection_matrix, ("dp", "sp"), axis=0, tiled=True)
    position, target = routing_plan(block_dest, block_count, sp_count, peer_most)
    local_values = jnp.dot(tokens, weight_full, preferred_element_type=jnp.float32).astype(
        jnp.bfloat16
    )
    packed, labels = pack_blocks(
        local_values.reshape(block_count, block_rows, -1), position, target, dp_count, peer_most
    )
    received, got_labels = (
        lax.all_to_all(packed, "dp", split_axis=0, concat_axis=0, tiled=True),
        lax.all_to_all(labels, "dp", split_axis=0, concat_axis=0, tiled=True),
    )
    arrived = got_labels.reshape(-1).astype(jnp.float32).astype(jnp.int32)
    projected_values = unpack_blocks(received, arrived, block_count, block_rows)
    head_queries, head_keys, head_values, head_grads = (
        lax.all_to_all(queries, "sp", split_axis=1, concat_axis=0, tiled=True),
        lax.all_to_all(rotated_key_rows, "sp", split_axis=1, concat_axis=0, tiled=True),
        lax.all_to_all(projected_values, "sp", split_axis=1, concat_axis=0, tiled=True),
        lax.all_to_all(output_cotangent, "sp", split_axis=1, concat_axis=0, tiled=True),
    )
    query_part, key_part, value_part = attend_local(
        head_queries, head_keys, head_values, head_grads, doc_ids[0]
    )
    query_gradient, key_gradient, value_rows = (
        lax.all_to_all(query_part, "sp", split_axis=0, concat_axis=1, tiled=True),
        lax.all_to_all(key_part, "sp", split_axis=0, concat_axis=1, tiled=True),
        lax.all_to_all(value_part, "sp", split_axis=0, concat_axis=1, tiled=True),
    )
    value_feature_width = value_rows.shape[1]
    grad_blocks = value_rows.reshape(block_count, block_rows, value_feature_width)
    valid = arrived >= 0
    backward = jnp.where(
        valid[:, None, None], grad_blocks[jnp.maximum(arrived, 0)], jnp.zeros((), jnp.bfloat16)
    )
    backward = backward.reshape(dp_count, peer_most * block_rows, value_feature_width)
    returned = lax.all_to_all(backward, "dp", split_axis=0, concat_axis=0, tiled=True)
    grad_rows = returned.reshape(-1, block_rows, value_feature_width)[position].reshape(
        tok_count, value_feature_width
    )
    weight_grad = lax.psum_scatter(
        lax.dot_general(
            tokens, grad_rows, (((0,), (0,)), ((), ())), preferred_element_type=jnp.float32
        ),
        ("dp", "sp"),
        scatter_dimension=0,
        tiled=True,
    )
    return (query_gradient, key_gradient, weight_grad)


def solution(mesh):
    in_specs = (
        P(("dp", "sp"), None),
        P(("dp", "sp"), None),
        P(("dp", "sp"), None),
        P(("dp", "sp"), None),
        P(("dp", "sp"), None),
        P(("dp", "sp")),
        P("dp", None),
    )
    out_specs = (P(("dp", "sp"), None), P(("dp", "sp"), None), P(("dp", "sp"), None))
    return jax.shard_map(
        per_device, mesh=mesh, in_specs=in_specs, out_specs=out_specs, check_vma=False
    )
```

profile of v0, /device:TPU:0, one launch (start us, length us, event | category | flops | bytes accessed | tf_op | source)
XLA Modules:
  0.0 986.5 jit_solution(3563886635680287838)
XLA Ops:
  10.2 8.4 all-to-all-start.4
  18.6 1.8 copy.110
  20.4 5.5 all-to-all-done.4
  25.9 4.3 all-to-all-start.1
  30.2 3.1 copy.162
  33.3 3.6 all-to-all-done.1
  37.7 3.6 all-to-all-start
  41.3 51.5 %all-gather.2.cloned.1.call-done = bf16[8192,512]{1,0:T(8,128)(2,1)} async-done(((bf16[64,512]{1,0:T(8,128)(2,1)}), bf16[8192,512]{1,0:T(8,128)(2,1)}) %all-gather.2.cloned.1.call-update) | async-done | bytes 8388624 | tf_op jit(solution)/shard_map/all_gather | solution.py:119
  92.7 7.0 fusion.42
  100.6 3.8 scatter_fusion
  104.4 4.7 all-to-all-start.3
  109.1 3.1 copy.161
  112.2 8.6 all-to-all-done.3
  120.9 4.4 all-to-all-start.2
  128.2 24.0 %all-to-all-done.2 = bf16[256,4,1024]{2,0,1:T(8,128)(2,1)} async-done(((bf16[256,4,1024]{2,0,1:T(8,128)(2,1)}), bf16[256,4,1024]{2,0,1:T(8,128)(2,1)}, u32[]{:S(2)}, u32[]{:S(2)}) %all-to-all-start.2) | async-done | bytes 2097184 | tf_op jit(solution)/shard_map/all_to_all | solution.py:137
  152.2 3.4 all-to-all-start.5
  157.6 2.0 copy.148
  159.5 3.5 copy.149
  163.9 82.2 %while.15 = (s32[]{:T(128)}, f32[1024,1,128]{0,2,1:T(8,128)S(1)}, f32[1024,1,128]{0,2,1:T(8,128)}, bf16[2,512,1024]{2,1,0:T(8,128)(2,1)}, bf16[2,512,1,8,128]{4,...) while((s32[]{:T(128)}, f32[1024,1,128]{0,2,1:T(8,128)S(1)}, ...), condition=%wide.region_8.9_spmd.clone, body=%wide.region_4.8_spmd.clone.sunk | while | flops 6547821056 | bytes 204667184 | solution.py:94
  166.1 1.7 constant_dynamic-slice_fusion.3
  167.8 1.5 copy.173
  169.3 3.3 fusion.75
  172.7 4.5 fusion.76
  177.2 5.9 fusion.77
  183.1 6.5 fusion.80
  189.6 9.2 fusion.78
  198.8 1.3 fusion.79
  200.1 2.9 multiply_convert_fusion.3
  206.6 1.7 constant_dynamic-slice_fusion.3
  208.3 1.5 copy.173
  209.8 3.3 fusion.75
  213.1 4.5 fusion.76
  217.7 5.9 fusion.77
  223.6 7.6 fusion.80
  231.1 9.2 fusion.78
  241.7 2.9 multiply_convert_fusion.3
  248.0 4.8 all-to-all-start.8
  253.0 6.5 all-to-all-done.8
  261.3 3.9 all-to-all-start.9
  265.3 11.7 %all-to-all-done.9 = bf16[32,16,512]{2,1,0:T(8,128)(2,1)S(1)} async-done(((bf16[32,16,512]{2,1,0:T(8,128)(2,1)}), bf16[32,16,512]{2,1,0:T(8,128)(2,1)S(1)}, u32[]{:S(2)}, u32[]{:S(2)}) %all-to-all-start.9) | async-done | bytes 524320 | tf_op jit(solution)/shard_map/all_to_all | solution.py:154
  277.6 10.3 %convolution_bitcast_fusion = f32[8192,512]{0,1:T(8,128)} fusion(bf16[256,8192]{1,0:T(8,128)(2,1)} %param.9, bf16[32,8,512]{2,1,0:T(8,128)(2,1)S(1)} %gather_fusion.2), kind=kOutput, calls=%fused_computation.44 | convolution fusion | flops 2147483648 | bytes 21233664 | tf_op jit(solution)/shard_map/dot_general | solution.py:159
  287.9 17.4 %copy.138 = f32[8192,512]{1,0:T(8,128)} copy(f32[8192,512]{0,1:T(8,128)} %convolution_bitcast_fusion) | data formatting | bytes 33554432
  305.6 11.1 %all_to_all.134 = bf16[4,256,128]{2,1,0:T(8,128)(2,1)S(1)} all-to-all(bf16[4,256,128]{2,1,0:T(8,128)(2,1)S(1)} %bitcast.251), channel_id=1, replica_groups=mesh['dp'=32,'sp'=4] {'sp'}, dimensions={0} | all-to-all | bytes 524288 | tf_op jit(solution)/shard_map/all_to_all | solution.py:144
  316.7 3.6 all-to-all-start.6
  321.3 31.1 %all-to-all-done.6 = bf16[4,256,1024]{2,1,0:T(8,128)(2,1)S(1)} async-done(((bf16[4,256,1024]{2,1,0:T(8,128)(2,1)}), bf16[4,256,1024]{2,1,0:T(8,128)(2,1)S(1)}, u32[]{:S(2)}, u32[]{:S(2)}) %all-to-all-start.6) | async-done | bytes 2097184 | tf_op jit(solution)/shard_map/all_to_all | solution.py:143
  352.4 2.5 copy.120
  355.0 4.1 copy.127
  359.1 620.6 %reduce-scatter.4.cloned.1.call-done = f32[64,512]{1,0:T(8,128)} async-done(((f32[8192,512]{1,0:T(8,128)}), f32[64,512]{1,0:T(8,128)}) %reduce-scatter.4.cloned.1.call-update) | async-done | bytes 131088
  (83 shorter events, 23.1 us)
Async XLA Ops:
  7.2 85.6 %all-gather.2.cloned.1.call-start = ((), (), s32[]{:S(2)}) async-start(), calls=%async_computation.11 | async-start | bytes 8454144 | tf_op jit(solution)/shard_map/all_gather | solution.py:119
  8.8 91.8 %copy-start.7 = (s32[32]{0:T(128)}, s32[32]{0:T(128)S(1)}, u32[]{:S(2)}) copy-start(s32[32]{0:T(128)S(1)} %compare_select_fusion.1) | copy-start | bytes 388
  10.2 15.7 %all-to-all-start.4 = ((bf16[32,1,2]{2,1,0:T(2,128)(2,1)}), bf16[32,1,2]{2,1,0:T(2,128)(2,1)S(1)}, u32[]{:S(2)}, u32[]{:S(2)}) async-start(bf16[32,1,2]{2,1,0:T(2,128)(2,1)} %convert_element_type.126), calls=%async_computation.4 | async-start | bytes 32768 | tf_op jit(solution)/shard_map/all_to_all | solution.py:129
  25.9 11.1 %all-to-all-start.1 = ((bf16[256,4,128]{0,2,1:T(8,128)(2,1)}), bf16[256,4,128]{0,2,1:T(8,128)(2,1)S(1)}, u32[]{:S(2)}, u32[]{:S(2)}) async-start(bf16[256,4,128]{0,2,1:T(8,128)(2,1)} %bitcast.2), calls=%async_computation.1 | async-start | bytes 524288 | tf_op jit(solution)/shard_map/all_to_all | solution.py:135
  37.0 0.7 copy-start.2
  37.7 66.7 %all-to-all-start = ((bf16[256,4,1024]{2,0,1:T(8,128)(2,1)}), bf16[256,4,1024]{2,0,1:T(8,128)(2,1)S(1)}, u32[]{:S(2)}, u32[]{:S(2)}) async-start(bf16[256,4,1024]{2,0,1:T(8,128)(2,1)} %bitcast.239), calls=%async_computation | async-start | bytes 4194304 | tf_op jit(solution)/shard_map/all_to_all | solution.py:134
  104.4 16.5 %all-to-all-start.3 = ((bf16[32,16,512]{2,1,0:T(8,128)(2,1)}), bf16[32,16,512]{2,1,0:T(8,128)(2,1)S(1)}, u32[]{:S(2)}, u32[]{:S(2)}) async-start(bf16[32,16,512]{2,1,0:T(8,128)(2,1)} %bitcast.7), calls=%async_computation.3 | async-start | bytes 1048576 | tf_op jit(solution)/shard_map/all_to_all | solution.py:128
  112.2 51.7 %copy-start.4 = (s32[1,1024]{1,0:T(1,128)S(1)}, s32[1,1024]{1,0:T(1,128)}, u32[]{:S(2)}) copy-start(s32[1,1024]{1,0:T(1,128)} %param.15) | copy-start | bytes 12292
  120.9 31.3 %all-to-all-start.2 = ((bf16[256,4,1024]{2,0,1:T(8,128)(2,1)}), bf16[256,4,1024]{2,0,1:T(8,128)(2,1)}, u32[]{:S(2)}, u32[]{:S(2)}) async-start(bf16[256,4,1024]{2,0,1:T(8,128)(2,1)} %bitcast.238), calls=%async_computation.2 | async-start | bytes 4194304 | tf_op jit(solution)/shard_map/all_to_all | solution.py:137
  152.2 10.8 %all-to-all-start.5 = ((bf16[256,4,128]{2,0,1:T(8,128)(2,1)}), bf16[256,4,128]{2,0,1:T(8,128)(2,1)S(1)}, u32[]{:S(2)}, u32[]{:S(2)}) async-start(bf16[256,4,128]{2,0,1:T(8,128)(2,1)} %copy.114), calls=%async_computation.5 | async-start | bytes 524288 | tf_op jit(solution)/shard_map/all_to_all | solution.py:136
  163.9 88.9 %copy-start.6 = (pred[32,1,2]{0,2,1:T(4,128)(4,1)S(1)}, pred[32,1,2]{0,2,1:T(4,128)(4,1)}, u32[]{:S(2)}) copy-start(pred[32,1,2]{0,2,1:T(4,128)(4,1)} %copy.123) | copy-start | bytes 196
  163.9 89.0 %copy-start.5 = (s32[32,2]{1,0:T(8,128)S(1)}, s32[32,2]{1,0:T(8,128)}, u32[]{:S(2)}) copy-start(s32[32,2]{1,0:T(8,128)} %get-tuple-element.183) | copy-start | bytes 772
  163.9 101.4 %copy-start.8 = (s32[32]{0:T(128)S(1)}, s32[32]{0:T(128)}, u32[]{:S(2)}) copy-start(s32[32]{0:T(128)} %copy-done.7) | copy-start | bytes 388
  172.6 10.4 %copy-start = (f32[512,8,1024]{2,0,1:T(8,128)}, f32[512,8,1024]{2,0,1:T(8,128)S(1)}, u32[]{:S(2)}) copy-start(f32[512,8,1024]{2,0,1:T(8,128)S(1)} %get-tuple-element.286) | copy-start | bytes 50331652 | tf_op jit(solution)/shard_map/while
  172.6 4.5 copy-start.1
  172.6 4.5 copy-start.3
  213.1 10.4 %copy-start = (f32[512,8,1024]{2,0,1:T(8,128)}, f32[512,8,1024]{2,0,1:T(8,128)S(1)}, u32[]{:S(2)}) copy-start(f32[512,8,1024]{2,0,1:T(8,128)S(1)} %get-tuple-element.286) | copy-start | bytes 50331652 | tf_op jit(solution)/shard_map/while
  213.1 4.5 copy-start.1
  213.1 4.5 copy-start.3
  248.0 11.4 %all-to-all-start.8 = ((bf16[4,256,128]{2,1,0:T(8,128)(2,1)}), bf16[4,256,128]{2,1,0:T(8,128)(2,1)S(1)}, u32[]{:S(2)}, u32[]{:S(2)}) async-start(bf16[4,256,128]{2,1,0:T(8,128)(2,1)} %bitcast.19), calls=%async_computation.8 | async-start | bytes 524288 | tf_op jit(solution)/shard_map/all_to_all | solution.py:145
  261.3 15.7 %all-to-all-start.9 = ((bf16[32,16,512]{2,1,0:T(8,128)(2,1)}), bf16[32,16,512]{2,1,0:T(8,128)(2,1)S(1)}, u32[]{:S(2)}, u32[]{:S(2)}) async-start(bf16[32,16,512]{2,1,0:T(8,128)(2,1)} %bitcast_select_fusion.1), calls=%async_computation.9 | async-start | bytes 1048576 | tf_op jit(solution)/shard_map/all_to_all | solution.py:154
  265.2 714.5 %reduce-scatter.4.cloned.1.call-start = ((), (), s32[]{:S(2)}) async-start(), calls=%async_computation.12 | async-start | bytes 16908288
  316.7 35.7 %all-to-all-start.6 = ((bf16[4,256,1024]{2,1,0:T(8,128)(2,1)}), bf16[4,256,1024]{2,1,0:T(8,128)(2,1)S(1)}, u32[]{:S(2)}, u32[]{:S(2)}) async-start(bf16[4,256,1024]{2,1,0:T(8,128)(2,1)} %bitcast.244), calls=%async_computation.6 | async-start | bytes 4194304 | tf_op jit(solution)/shard_map/all_to_all | solution.py:143
Sparse Core Ops, SparseCore 0:
  11.1 81.5 all-gather.1
  305.4 674.1 reduce-scatter.3
where the time goes:
time: 988 us; the launch traced here: 987 us
  waiting for transfers between devices  764 us (77%)
  matrix products  76.5 us (8%)
  local copies, waits for them, and re-layouts  63.3 us (6%)
  starting transfers between devices  41.2 us (4%)
  other arithmetic  14.5 us (1%)
  between operations  14.3 us (1%)
  blocking collectives  11.1 us (1%)
    unnamed x3, waiting for transfers between devices  621 us
    all_gather x1, waiting for transfers between devices, per_device(): lax.all_gather(value_projection_matrix, ('dp', 'sp'), axis=0, tiled=True)  51.5 us
    unnamed x20, local copies, waits for them, and re-layouts  31.4 us
    all_to_all x1, waiting for transfers between devices, per_device(): lax.all_to_all(query_part, 'sp', split_axis=0, concat_axis=1, tiled=True)  31.1 us
    all_to_all x1, waiting for transfers between devices, per_device(): lax.all_to_all(output_cotangent, 'sp', split_axis=1, concat_axis=0, tiled...  24 us
  transfers between devices with their start and end apart: 11, of which 9 were waited for; matrix products, arithmetic and copies ran while one was open for 4% of the time, Pallas kernels for 0%

commit v1 on v0

v1 whole, which is shorter than its diff:
```python
import functools
import math

import jax
import jax.numpy as jnp
from jax import lax
from jax.experimental import pallas as pl
from jax.experimental.pallas import tpu as pltpu
from jax.sharding import PartitionSpec as P

MESH = pl.DeviceIdType.MESH
BF = jnp.bfloat16
F32 = jnp.float32
HEADS = 32
KV_HEADS = 4
HEAD = 128
ROWS = 256
KEYS = 1024
FEAT = 512
SLOTS = 512
BLK = 8
SCALE = 1.0 / math.sqrt(HEAD)
LOG2E = math.log2(math.e)


def nn(a, b):
    return lax.dot_general(a, b, (((1,), (0,)), ((), ())), preferred_element_type=F32)


def nt(a, b):
    return lax.dot_general(a, b, (((1,), (1,)), ((), ())), preferred_element_type=F32)


def tn(a, b):
    return lax.dot_general(a, b, (((0,), (0,)), ((), ())), preferred_element_type=F32)


def kernel(
    tok_hbm, w_hbm, q_hbm, k_hbm, do_hbm, pos_ref, lab_ref, doc_ref,
    dq_hbm, dk_ref, wg_ref,
    tok, wh, qv, dov, dqv, kf, kt, vf, prob, inv_row, bias, acc, part, part_in,
    snd, rcv, lsnd, lrcv, fwd, bwd_t, bsnd, brcv, dvl,
    gsend, gin, f1a, f2a, f1b, f2b, mpa, mma, mpb, mmb, s2a, s2b, s3,
    loc_sem, tl_sem, ts_sem, tr_sem, wx_s, wx_r, w2_s, w2_r, w3_s, w3_r, k_s, k_r,
    l_s, l_r, a_s, a_r, b_s, b_r, p_s, p_r, d_s, d_r, v_s, v_r, dv_s, dv_r, dk_s, dk_r,
    g_s, g_r, g2_s, g2_r, g3_s, g3_r, dq_s,
):
    me = lax.axis_index("dp")
    x = lax.axis_index("sp")
    z, y, c = me // 8, (me // 2) % 4, me % 2

    def at(zz, yy, xx):
        return (zz * 8 + yy * 2 + c, xx)

    def up(v, o):
        return (v + o) % 4

    def along_x(o):
        return at(z, y, up(x, o))

    def along_y(o):
        return at(z, up(y, o), x)

    def along_z(o):
        return at(up(z, o), y, x)

    sibling = (z * 8 + y * 2 + (1 - c), x)

    def remote(src, dst, ss, rs, dev):
        return pltpu.make_async_remote_copy(src, dst, ss, rs, device_id=dev, device_id_type=MESH)

    own_w = pltpu.make_async_copy(w_hbm, wh.at[z, y, pl.ds(x * 64, 64)], loc_sem.at[0])
    own_k = pltpu.make_async_copy(k_hbm, kf.at[pl.ds(x * ROWS, ROWS)], loc_sem.at[1])
    own_q = pltpu.make_async_copy(q_hbm, qv, loc_sem.at[2])
    own_do = pltpu.make_async_copy(do_hbm, dov, loc_sem.at[3])
    own_w.start()
    own_k.start()
    own_q.start()
    own_do.start()

    def tok_local(i):
        return pltpu.make_async_copy(
            tok_hbm.at[:, pl.ds((i * 2 + c) * 256, 256)],
            tok.at[pl.ds(0, ROWS), pl.ds(i * 256, 256)], tl_sem.at[i])

    def tok_remote(i):
        return remote(
            tok_hbm.at[:, pl.ds((i * 2 + 1 - c) * 256, 256)],
            tok.at[pl.ds(ROWS, ROWS), pl.ds(i * 256, 256)], ts_sem.at[i], tr_sem.at[i], sibling)

    barrier = pltpu.get_barrier_semaphore()

    def greet(o, carry):
        pl.semaphore_signal(barrier, inc=1, device_id=((me + o) % 32, x), device_id_type=MESH)
        return carry

    lax.fori_loop(1, 32, greet, 0)
    for o in (1, 2, 3):
        pl.semaphore_signal(barrier, inc=1, device_id=along_x(o), device_id_type=MESH)
    pl.semaphore_wait(barrier, 34)

    def w_x(o):
        return remote(w_hbm, wh.at[z, y, pl.ds(x * 64, 64)], wx_s.at[o], wx_r.at[o], along_x(o))

    def k_x(o, e):
        i = (o - 1) * 4 + e
        cols = pl.ds(e * HEAD, HEAD)
        return remote(k_hbm.at[:, cols], kf.at[pl.ds(x * ROWS, ROWS), cols], k_s.at[i], k_r.at[i], along_x(o))

    for o in (1, 3, 2):
        w_x(o).start()
    for e in range(KV_HEADS):
        for o in (1, 3, 2):
            k_x(o, e).start()

    r_i = lax.broadcasted_iota(jnp.int32, (SLOTS, ROWS), 0)
    c_i = lax.broadcasted_iota(jnp.int32, (SLOTS, ROWS), 1)
    same_row = (r_i % BLK) == (c_i % BLK)
    fwd[...] = jnp.where(same_row & ((r_i // BLK) == pos_ref[0:1, :]), 1.0, 0.0).astype(BF)
    lsnd[...] = nn(fwd[...], lab_ref[...]).astype(BF)

    def peers(send_buf, recv_buf, ss, rs):
        def one(o):
            p = (me + o) % 32
            return remote(send_buf.at[pl.ds(p * 16, 16)], recv_buf.at[pl.ds(me * 16, 16)], ss.at[o], rs.at[o], (p, x))

        def start():
            def body(o, carry):
                one(o).start()
                return carry

            lax.fori_loop(1, 32, body, 0)
            mine = pl.ds(pl.multiple_of(me * 16, 16), 16)
            recv_buf[mine, :] = send_buf[mine, :]

        def wait_recv():
            def body(o, carry):
                one(o).wait_recv()
                return carry

            lax.fori_loop(1, 32, body, 0)

        def wait_send():
            def body(o, carry):
                one(o).wait_send()
                return carry

            lax.fori_loop(1, 32, body, 0)

        return start, wait_recv, wait_send

    l_start, l_recv, l_done = peers(lsnd, lrcv, l_s, l_r)
    a_start, a_recv, a_done = peers(snd, rcv, a_s, a_r)
    b_start, b_recv, b_done = peers(bsnd, brcv, b_s, b_r)
    l_start()

    def start_tokens(i, carry):
        tok_local(i).start()
        tok_remote(i).start()
        return carry

    lax.fori_loop(0, 16, start_tokens, 0)

    cut = jnp.sum(jnp.where(doc_ref[0:1, :] == 0, 1, 0), axis=1, keepdims=True)
    k_pos = lax.broadcasted_iota(jnp.int32, (KEYS, ROWS), 0)
    q_pos = lax.broadcasted_iota(jnp.int32, (KEYS, ROWS), 1) + x * ROWS
    allowed = (k_pos <= q_pos) & ((k_pos < cut) == (q_pos < cut))
    bias[...] = jnp.where(allowed, 0.0, -1e30)

    def w_2a(o):
        blk = wh.at[z, y, pl.ds(0, 128)]
        return remote(blk, blk, w2_s.at[o], w2_r.at[o], along_y(o))

    def w_2b(o):
        blk = wh.at[z, y, pl.ds(128, 128)]
        return remote(blk, blk, w2_s.at[4 + o], w2_r.at[4 + o], along_z(o))

    def w_3a(j, m):
        yy = up(y, j)
        if m < 2:
            blk = wh.at[z, yy, pl.ds(0, 128)]
        elif m == 2:
            blk = wh.at[up(z, 3), yy, pl.ds(0, 64)]
        else:
            blk = wh.at[up(z, 1), yy, pl.ds(64, 64)]
        i = j * 4 + m
        return remote(blk, blk, w3_s.at[i], w3_r.at[i], along_z(1 if m % 2 == 0 else 3))

    def w_3b(j, m):
        zz = up(z, j)
        if m < 2:
            blk = wh.at[zz, y, pl.ds(128, 128)]
        elif m == 2:
            blk = wh.at[zz, up(y, 3), pl.ds(128, 64)]
        else:
            blk = wh.at[zz, up(y, 1), pl.ds(192, 64)]
        i = 16 + j * 4 + m
        return remote(blk, blk, w3_s.at[i], w3_r.at[i], along_y(1 if m % 2 == 0 else 3))

    def w_begin():
        own_w.wait()
        for o in (1, 3, 2):
            w_x(o).wait_recv()
        for o in (1, 3, 2):
            w_2a(o).start()
            w_2b(o).start()
        for m in (0, 1):
            w_3a(0, m).start()
            w_3b(0, m).start()

    def w_full(j):
        w_2a((4 - j) % 4).wait_recv()
        w_2b((4 - j) % 4).wait_recv()
        for m in (0, 1):
            w_3a(j, m).start()
            w_3b(j, m).start()

    def w_forward(j):
        for m in (0, 1):
            w_3a(j, m).wait_recv()
            w_3a(j, m + 2).start()
            w_3b(j, m).wait_recv()
            w_3b(j, m + 2).start()

    def w_end():
        for j in (0, 1, 3, 2):
            for m in (2, 3):
                w_3a(j, m).wait_recv()
                w_3b(j, m).wait_recv()
        for o in (1, 2, 3):
            w_x(o).wait_send()
            w_2a(o).wait_send()
            w_2b(o).wait_send()
        for j in range(4):
            for m in range(4):
                w_3a(j, m).wait_send()
                w_3b(j, m).wait_send()

    def sum_x(ss, rs):
        def one(o, e):
            i = (o - 1) * 4 + e
            cols = pl.ds(e * HEAD, HEAD)
            return remote(gsend.at[pl.ds(up(x, o) * ROWS, ROWS), cols], gin.at[o - 1, :, cols], ss.at[i], rs.at[i], along_x(o))

        def start(e):
            cols = pl.ds(e * HEAD, HEAD)
            gsend[:, cols] = acc[:, cols].astype(BF)
            for o in (1, 3, 2):
                one(o, e).start()

        def finish():
            for e in range(KV_HEADS):
                for o in (1, 3, 2):
                    one(o, e).wait_recv()
            own = acc[pl.ds(pl.multiple_of(x * ROWS, ROWS), ROWS), :]
            total = own + gin[0].astype(F32) + gin[1].astype(F32) + gin[2].astype(F32)
            for e in range(KV_HEADS):
                for o in (1, 3, 2):
                    one(o, e).wait_send()
            return total

        return start, finish

    dv_start, dv_finish = sum_x(dv_s, dv_r)
    dk_start, dk_finish = sum_x(dk_s, dk_r)

    def at_head(h, where, act):
        pl.when(h == where)(act)

    w_begin()
    own_q.wait()
    own_do.wait()
    own_k.wait()

    def first(h, carry):
        e = h // 8
        for i in range(KV_HEADS):
            @pl.when(h == 8 * i)
            def _():
                for o in (1, 3, 2):
                    k_x(o, i).wait_recv()
        at_head(h, 3, lambda: w_full(1))
        at_head(h, 5, lambda: w_full(3))
        at_head(h, 7, lambda: w_full(2))
        at_head(h, 11, lambda: w_forward(0))
        at_head(h, 16, lambda: w_forward(1))
        at_head(h, 22, lambda: w_forward(3))
        at_head(h, 28, lambda: w_forward(2))
        ecol = pl.ds(pl.multiple_of(e * HEAD, HEAD), HEAD)
        hcol = pl.ds(pl.multiple_of(h * HEAD, HEAD), HEAD)
        s = nt(kf[:, ecol], qv[:, hcol]) * (SCALE * LOG2E) + bias[...]
        m = jnp.max(s, axis=0, keepdims=True)
        p = jnp.exp2(s - m)
        inv = 1.0 / jnp.sum(p, axis=0, keepdims=True)
        low = p.astype(BF)
        prob[h] = low
        inv_row[h] = inv
        inv_rows = jnp.transpose(jnp.broadcast_to(inv, (HEAD, ROWS)))
        do = (dov[:, hcol].astype(F32) * inv_rows).astype(BF)
        dov[:, hcol] = do
        add = nn(low, do)

        @pl.when(h % 8 == 0)
        def _():
            acc[:, ecol] = add

        @pl.when(h % 8 != 0)
        def _():
            acc[:, ecol] += add

        for i in range(KV_HEADS):
            at_head(h, 8 * i + 7, lambda i=i: dv_start(i))
        return carry

    lax.fori_loop(0, HEADS, first, 0)

    l_recv()
    lab = lrcv[...].astype(F32)
    want = (c_i // BLK + 1).astype(F32)
    bwd_t[...] = jnp.where(same_row & (jnp.concatenate([lab, lab], axis=1) == want), 1.0, 0.0).astype(BF)
    bsnd[...] = nn(bwd_t[...], dv_finish().astype(BF)).astype(BF)
    b_start()

    def tokens_in(i, carry):
        tok_local(i).wait()
        tok_remote(i).wait_recv()
        return carry

    lax.fori_loop(0, 16, tokens_in, 0)
    w_end()

    def project(first_row):
        total = None
        for zz in range(4):
            term = nn(tok[pl.ds(first_row, ROWS), pl.ds(zz * 1024, 1024)], wh[zz].reshape(1024, FEAT))
            total = term if total is None else total + term
        return total

    give_part = remote(part, part_in, p_s.at[0], p_r.at[0], sibling)
    part[...] = project(ROWS)
    give_part.start()
    mine = project(0)
    give_part.wait_recv()
    values = (mine + part_in[...]).astype(BF)
    snd[...] = nn(fwd[...], values).astype(BF)
    a_start()

    b_recv()
    dvl[pl.ds(0, ROWS), :] = tn(fwd[...], brcv[...]).astype(BF)
    give_dvl = remote(dvl.at[pl.ds(0, ROWS)], dvl.at[pl.ds(ROWS, ROWS)], d_s.at[0], d_r.at[0], sibling)
    give_dvl.start()
    give_dvl.wait_recv()

    def weight_block(i, carry):
        cols = pl.ds(pl.multiple_of(i * 256, 256), 256)
        wh[i // 4, i % 4] = tn(tok[:, cols], dvl[...]).astype(BF)
        return carry

    lax.fori_loop(0, 16, weight_block, 0)

    a_rows, b_rows = pl.ds(0, 128), pl.ds(128, 128)
    low2, high2 = pl.ds(0, 2), pl.ds(2, 2)

    g_1 = [
        remote(wh.at[up(z, 2), low2, a_rows], f1a, g_s.at[0], g_r.at[0], along_z(1)),
        remote(wh.at[up(z, 2), high2, a_rows], f2a, g_s.at[1], g_r.at[1], along_z(3)),
        remote(wh.at[low2, up(y, 2), b_rows], f1b, g_s.at[2], g_r.at[2], along_y(1)),
        remote(wh.at[high2, up(y, 2), b_rows], f2b, g_s.at[3], g_r.at[3], along_y(3)),
        remote(wh.at[up(z, 1), high2, a_rows], mpa.at[high2], g_s.at[4], g_r.at[4], along_z(1)),
        remote(wh.at[up(z, 3), low2, a_rows], mma.at[low2], g_s.at[5], g_r.at[5], along_z(3)),
        remote(wh.at[high2, up(y, 1), b_rows], mpb.at[high2], g_s.at[6], g_r.at[6], along_y(1)),
        remote(wh.at[low2, up(y, 3), b_rows], mmb.at[low2], g_s.at[7], g_r.at[7], along_y(3)),
    ]
    g_2 = [
        remote(wh.at[up(z, 1), low2, a_rows], mpa.at[low2], g_s.at[8], g_r.at[8], along_z(1)),
        remote(wh.at[up(z, 3), high2, a_rows], mma.at[high2], g_s.at[9], g_r.at[9], along_z(3)),
        remote(wh.at[low2, up(y, 1), b_rows], mpb.at[low2], g_s.at[10], g_r.at[10], along_y(1)),
        remote(wh.at[high2, up(y, 3), b_rows], mmb.at[high2], g_s.at[11], g_r.at[11], along_y(3)),
    ]

    def g_3a(o):
        return remote(wh.at[z, up(y, o), a_rows], s2a.at[o - 1], g2_s.at[o], g2_r.at[o], along_y(o))

    def g_3b(o):
        return remote(wh.at[up(z, o), y, b_rows], s2b.at[o - 1], g2_s.at[4 + o], g2_r.at[4 + o], along_z(o))

    def g_x(o):
        rows = pl.ds(up(x, o) * 64, 64)
        return remote(wh.at[z, y, rows], s3.at[o - 1], g3_s.at[o], g3_r.at[o], along_x(o))

    def bsum(*terms):
        total = terms[0].astype(F32)
        for t in terms[1:]:
            total = total + t.astype(F32)
        return total

    def g_step1():
        for i in range(4):
            g_1[i].wait_recv()
            if i == 0:
                wh[up(z, 1), 0:2, 0:128] = bsum(wh[up(z, 1), 0:2, 0:128], f1a[...]).astype(BF)
            elif i == 1:
                wh[up(z, 3), 2:4, 0:128] = bsum(wh[up(z, 3), 2:4, 0:128], f2a[...]).astype(BF)
            elif i == 2:
                wh[0:2, up(y, 1), 128:256] = bsum(wh[0:2, up(y, 1), 128:256], f1b[...]).astype(BF)
            else:
                wh[2:4, up(y, 3), 128:256] = bsum(wh[2:4, up(y, 3), 128:256], f2b[...]).astype(BF)
            g_2[i].start()

    def g_step2():
        for i in range(4, 8):
            g_1[i].wait_recv()
        for d in g_2:
            d.wait_recv()
        for i in range(4):
            wh[z, i, 0:128] = bsum(wh[z, i, 0:128], mpa[i], mma[i]).astype(BF)
            wh[i, y, 128:256] = bsum(wh[i, y, 128:256], mpb[i], mmb[i]).astype(BF)
        for o in (1, 3, 2):
            g_3a(o).start()
            g_3b(o).start()

    def g_step3():
        for o in (1, 3, 2):
            g_3a(o).wait_recv()
            g_3b(o).wait_recv()
        wh[z, y, 0:128] = bsum(wh[z, y, 0:128], s2a[0], s2a[1], s2a[2]).astype(BF)
        wh[z, y, 128:256] = bsum(wh[z, y, 128:256], s2b[0], s2b[1], s2b[2]).astype(BF)
        for o in (1, 3, 2):
            g_x(o).start()

    def g_step4():
        for o in (1, 3, 2):
            g_x(o).wait_recv()
        rows = pl.ds(pl.multiple_of(x * 64, 64), 64)
        wg_ref[...] = bsum(wh[z, y, rows, :], s3[0], s3[1], s3[2])
        for d in g_1 + g_2:
            d.wait_send()
        for o in (1, 2, 3):
            g_3a(o).wait_send()
            g_3b(o).wait_send()
            g_x(o).wait_send()

    for d in g_1:
        d.start()

    a_recv()
    mine_rows = pl.ds(pl.multiple_of(x * ROWS, ROWS), ROWS)
    vf[mine_rows, :] = tn(bwd_t[...], rcv[...]).astype(BF)

    def v_x(o, e):
        i = (o - 1) * 4 + e
        blk = vf.at[pl.ds(x * ROWS, ROWS), pl.ds(e * HEAD, HEAD)]
        return remote(blk, blk, v_s.at[i], v_r.at[i], along_x(o))

    for e in range(KV_HEADS):
        for o in (1, 3, 2):
            v_x(o, e).start()
    for e in range(KV_HEADS):
        kt[e] = jnp.transpose(kf[:, pl.ds(e * HEAD, HEAD)].astype(F32)).astype(BF)

    def dq_out(e):
        cols = pl.ds(e * 1024, 1024)
        return pltpu.make_async_copy(dqv.at[:, cols], dq_hbm.at[:, cols], dq_s.at[e])

    def second(h, carry):
        e = h // 8
        for i in range(KV_HEADS):
            @pl.when(h == 8 * i)
            def _():
                for o in (1, 3, 2):
                    v_x(o, i).wait_recv()
        at_head(h, 2, g_step1)
        at_head(h, 20, g_step2)
        at_head(h, 29, g_step3)
        ecol = pl.ds(pl.multiple_of(e * HEAD, HEAD), HEAD)
        hcol = pl.ds(pl.multiple_of(h * HEAD, HEAD), HEAD)
        do = dov[:, hcol]
        dp = nt(vf[:, ecol], do)
        p = prob[h].astype(F32)
        rd = jnp.sum(p * dp, axis=0, keepdims=True) * inv_row[h]
        ds = (p * (dp - rd)).astype(BF)
        add = nn(ds, qv[:, hcol])

        @pl.when(h % 8 == 0)
        def _():
            acc[:, ecol] = add

        @pl.when(h % 8 != 0)
        def _():
            acc[:, ecol] += add

        dq_t = nn(kt[e], ds) * SCALE
        dqv[:, hcol] = jnp.transpose(dq_t).astype(BF)
        for i in range(KV_HEADS):
            @pl.when(h == 8 * i + 7)
            def _():
                dk_start(i)
                dq_out(i).start()
        return carry

    lax.fori_loop(0, HEADS, second, 0)

    dk_ref[...] = (dk_finish() * SCALE).astype(BF)
    g_step4()

    for e in range(KV_HEADS):
        dq_out(e).wait()
        for o in (1, 2, 3):
            k_x(o, e).wait_send()
            v_x(o, e).wait_send()
    l_done()
    a_done()
    b_done()
    give_part.wait_send()
    give_dvl.wait_send()

    def tokens_out(i, carry):
        tok_remote(i).wait_send()
        return carry

    lax.fori_loop(0, 16, tokens_out, 0)


def per_device(tokens, w, queries, keys, cotangent, block_dest, doc_ids):
    dest_dp = block_dest // 128
    target = block_dest % 32
    earlier = jnp.arange(32)[None, :] < jnp.arange(32)[:, None]
    rank = jnp.sum(((dest_dp[None, :] == dest_dp[:, None]) & earlier).astype(jnp.int32), axis=1)
    pos = jnp.broadcast_to(jnp.repeat(dest_dp * 2 + rank, BLK)[None, :], (8, ROWS))
    lab = jnp.broadcast_to(jnp.repeat(target + 1, BLK)[:, None], (ROWS, 128)).astype(BF)
    doc = jnp.broadcast_to(doc_ids, (8, KEYS))
    vm = lambda shape, t: pltpu.VMEM(shape, t)
    dma = lambda n: pltpu.SemaphoreType.DMA((n,))
    anyspec = pl.BlockSpec(memory_space=pl.ANY)
    vspec = pl.BlockSpec(memory_space=pltpu.VMEM)
    scratch = [
        vm((512, 4096), BF),
        vm((4, 4, 256, FEAT), BF),
        vm((ROWS, 4096), BF),
        vm((ROWS, 4096), BF),
        vm((ROWS, 4096), BF),
        vm((KEYS, FEAT), BF),
        vm((KV_HEADS, HEAD, KEYS), BF),
        vm((KEYS, FEAT), BF),
        vm((HEADS, KEYS, ROWS), BF),
        vm((HEADS, 1, ROWS), F32),
        vm((KEYS, ROWS), F32),
        vm((KEYS, FEAT), F32),
        vm((ROWS, FEAT), F32),
        vm((ROWS, FEAT), F32),
        vm((SLOTS, FEAT), BF),
        vm((SLOTS, FEAT), BF),
        vm((SLOTS, 128), BF),
        vm((SLOTS, 128), BF),
        vm((SLOTS, ROWS), BF),
        vm((SLOTS, ROWS), BF),
        vm((SLOTS, FEAT), BF),
        vm((SLOTS, FEAT), BF),
        vm((512, FEAT), BF),
        vm((KEYS, FEAT), BF),
        vm((3, ROWS, FEAT), BF),
        vm((2, 128, FEAT), BF),
        vm((2, 128, FEAT), BF),
        vm((2, 128, FEAT), BF),
        vm((2, 128, FEAT), BF),
        vm((4, 128, FEAT), BF),
        vm((4, 128, FEAT), BF),
        vm((4, 128, FEAT), BF),
        vm((4, 128, FEAT), BF),
        vm((3, 128, FEAT), BF),
        vm((3, 128, FEAT), BF),
        vm((3, 64, FEAT), BF),
        dma(4), dma(16), dma(16), dma(16),
        dma(4), dma(4), dma(8), dma(8), dma(32), dma(32), dma(12), dma(12),
        dma(32), dma(32), dma(32), dma(32), dma(32), dma(32),
        dma(1), dma(1), dma(1), dma(1),
        dma(12), dma(12), dma(12), dma(12), dma(12), dma(12),
        dma(12), dma(12), dma(8), dma(8), dma(4), dma(4), dma(4),
    ]
    return pl.pallas_call(
        kernel,
        out_shape=(
            jax.ShapeDtypeStruct((ROWS, 4096), BF),
            jax.ShapeDtypeStruct((ROWS, FEAT), BF),
            jax.ShapeDtypeStruct((64, FEAT), F32),
        ),
        in_specs=[anyspec] * 5 + [vspec] * 3,
        out_specs=(anyspec, vspec, vspec),
        scratch_shapes=scratch,
        compiler_params=pltpu.CompilerParams(
            collective_id=0, has_side_effects=True, vmem_limit_bytes=62 * 1024 * 1024
        ),
        name="attention_and_weights",
    )(tokens, w, queries, keys, cotangent, pos, lab, doc)


def solution(mesh):
    both = P(("dp", "sp"), None)
    return jax.shard_map(
        per_device,
        mesh=mesh,
        in_specs=(both, both, both, both, both, P(("dp", "sp")), P("dp", None)),
        out_specs=(both, both, both),
        check_vma=False,
    )
```

time: 988 us -> 159 us (0.16)
  waiting for transfers between devices: 764 us -> 0 us
  Pallas kernels: 0 us -> 149 us
  matrix products: 76.5 us -> 0 us
  local copies, waits for them, and re-layouts: 63.3 us -> 7.52 us
  starting transfers between devices: 41.2 us -> 0 us
  other arithmetic: 14.5 us -> 0.85 us
  between operations: 14.3 us -> 0.67 us
  blocking collectives: 11.1 us -> 0 us
    unnamed x3 -> x0, waiting for transfers between devices: 621 us -> none
    pallas_call x0 -> x1, Pallas kernels: none -> 149 us  [per_device(): pl.pallas_call(kernel, out_shape=(jax.ShapeDtypeStruct((ROWS, 4096), BF),...]
    all_to_all x9 -> x0, waiting for transfers between devices: 91.1 us -> none  [the longest x1 31.1 us: per_device(): lax.all_to_all(query_part, 'sp', split_axis=0, concat_axis=1, tiled=True)]
    dot_general x14 -> x0, matrix products: 76.5 us -> none  [the longest x2 18.4 us: query_block(): jnp.einsum('qgrd,kgd->grqk', block_grads, value_three, preferred_element_...]
    all_gather x1 -> x0, waiting for transfers between devices: 51.5 us -> none  [per_device(): lax.all_gather(value_projection_matrix, ('dp', 'sp'), axis=0, tiled=True)]
    all_to_all x9 -> x0, starting transfers between devices: 41.1 us -> none  [the longest x1 8.42 us: per_device(): lax.all_to_all(labels, 'dp', split_axis=0, concat_axis=0, tiled=True)]
    unnamed x20 -> x7, local copies, waits for them, and re-layouts: 31.4 us -> 4.54 us
    all_to_all x1 -> x0, blocking collectives: 11.1 us -> none  [per_device(): lax.all_to_all(key_part, 'sp', split_axis=0, concat_axis=1, tiled=True)]
  transfers between devices with their start and end apart: 11 -> 0, of which waited for: 9 -> 0; matrix products, arithmetic and copies ran while one was open for 4% -> 0% of each run, Pallas kernels for 0% -> 0%
where the time goes in v1:
time: 159 us; the launch traced here: 158 us
  Pallas kernels  149 us (94%)
  local copies, waits for them, and re-layouts  7.52 us (5%)
    pallas_call x1, Pallas kernels, per_device(): pl.pallas_call(kernel, out_shape=(jax.ShapeDtypeStruct((ROWS, 4096), BF),...  149 us
    unnamed x7, local copies, waits for them, and re-layouts  4.54 us

profile of v1, /device:TPU:0, one launch (start us, length us, event | category | flops | bytes accessed | tf_op | source)
XLA Modules:
  0.0 158.3 jit_solution(7340721203722131736)
XLA Ops:
  0.6 0.7 fusion.2
  1.3 0.2 convert_reduce_fusion
  1.5 0.1 broadcast_in_dim.32
  1.6 0.1 convert_element_type.10
  1.7 0.1 broadcast_in_dim.14
  1.7 0.1 broadcast_in_dim.30
  1.8 0.6 broadcast_in_dim.31.pos_ref
  2.4 1.3 broadcast_in_dim.35.doc_ref
  3.7 0.7 broadcast_in_dim.33.lab_ref
  4.5 149.3 %attention_and_weights.1 = (bf16[256,4096]{1,0:T(8,128)(2,1)}, bf16[256,512]{1,0:T(8,128)(2,1)}, f32[64,512]{1,0:T(8,128)}) custom-call(bf16[256,8192]{1,0:T(8,128)(2,1)} %tok_hbm.1, bf16[64,512]{1,0:T(8,128)(2,1)} %w_hbm.1, bf16[256,4096]{1,0:T(8,128)(2,1)} %q_hbm.1, bf16[256,512]{1,0:T(8,128)(2,1)} %k_hbm.1, bf16[256,4096]{1,0:T(8,128)(2,1)} %do_hbm.1, ...), custom_call_target="tpu_custom_call" | custom-call | tf_op jit(solution)/shard_map/attention_and_weights/pallas_call | solution.py:580
  153.7 0.0 copy-start
  153.8 0.0 copy-start.1
  153.8 3.2 %copy.13 = bf16[256,4096]{1,0:T(8,128)(2,1)} copy(bf16[256,4096]{1,0:T(8,128)(2,1)} %get-tuple-element.8) | data formatting | bytes 4194304
  156.9 0.0 copy-done
  156.9 0.7 copy.14
  157.6 0.0 copy-done.1
  157.6 0.7 copy.15
  (1 shorter events, 0.0 us)
Async XLA Ops:
  153.7 3.2 %copy-start = (bf16[256,512]{1,0:T(8,128)(2,1)S(1)}, bf16[256,512]{1,0:T(8,128)(2,1)}, u32[]{:S(2)}) copy-start(bf16[256,512]{1,0:T(8,128)(2,1)} %get-tuple-element.9) | copy-start | bytes 786436
  153.8 3.9 %copy-start.1 = (f32[64,512]{1,0:T(8,128)S(1)}, f32[64,512]{1,0:T(8,128)}, u32[]{:S(2)}) copy-start(f32[64,512]{1,0:T(8,128)} %get-tuple-element.10) | copy-start | bytes 393220

commit v2 on v1

v2 whole, which is shorter than its diff:
```python
import functools
import math

import jax
import jax.numpy as jnp
from jax import lax
from jax.experimental import pallas as pl
from jax.experimental.pallas import tpu as pltpu
from jax.sharding import PartitionSpec as P

MESH = pl.DeviceIdType.MESH
BF = jnp.bfloat16
F32 = jnp.float32
HEADS = 32
KV_HEADS = 4
HEAD = 128
ROWS = 256
KEYS = 1024
FEAT = 512
SLOTS = 512
BLK = 8
SCALE = 1.0 / math.sqrt(HEAD)
LOG2E = math.log2(math.e)


def nn(a, b):
    return lax.dot_general(a, b, (((1,), (0,)), ((), ())), preferred_element_type=F32)


def nt(a, b):
    return lax.dot_general(a, b, (((1,), (1,)), ((), ())), preferred_element_type=F32)


def tn(a, b):
    return lax.dot_general(a, b, (((0,), (0,)), ((), ())), preferred_element_type=F32)


def kernel(
    tok_hbm, w_hbm, q_hbm, k_hbm, do_hbm, dest_ref, doc_ref,
    dq_hbm, dk_ref, wg_ref,
    tok, wh, qs, dos, kf, kt, vf, prob, inv_row, bias, acc, part, part_in,
    snd, rcv, lsnd, lrcv, fwd, bwd_t, bsnd, brcv, dvl,
    gsend, gin, f1a, f2a, f1b, f2b, mpa, mma, mpb, mmb, s2a, s2b, s3,
    loc_sem, q_sem, do_sem, tl_sem, ts_sem, tr_sem, wx_s, wx_r, w2_s, w2_r, w3_s, w3_r, k_s, k_r,
    l_s, l_r, a_s, a_r, b_s, b_r, p_s, p_r, d_s, d_r, v_s, v_r, dv_s, dv_r, dk_s, dk_r,
    g_s, g_r, g2_s, g2_r, g3_s, g3_r, dq_s, relay,
):
    me = lax.axis_index("dp")
    x = lax.axis_index("sp")
    z, y, c = me // 8, (me // 2) % 4, me % 2

    def at(zz, yy, xx):
        return (zz * 8 + yy * 2 + c, xx)

    def up(v, o):
        return (v + o) % 4

    def along_x(o):
        return at(z, y, up(x, o))

    def along_y(o):
        return at(z, up(y, o), x)

    def along_z(o):
        return at(up(z, o), y, x)

    sibling = (z * 8 + y * 2 + (1 - c), x)

    def remote(src, dst, ss, rs, dev):
        return pltpu.make_async_remote_copy(src, dst, ss, rs, device_id=dev, device_id_type=MESH)

    def landed(ref, sem):
        pltpu.make_async_copy(ref, ref, sem).wait()

    own_w = pltpu.make_async_copy(w_hbm, wh.at[z, y, pl.ds(x * 64, 64)], loc_sem.at[0])
    own_k = pltpu.make_async_copy(k_hbm, kf.at[pl.ds(x * ROWS, ROWS)], loc_sem.at[1])

    def head_in(src, dst, sem, h):
        return pltpu.make_async_copy(
            src.at[:, pl.ds(h * HEAD, HEAD)], dst.at[h // 8, pl.ds((h % 8) * ROWS, ROWS)], sem.at[h // 8])

    def q_in(h):
        return head_in(q_hbm, qs, q_sem, h)

    def do_in(h):
        return head_in(do_hbm, dos, do_sem, h)

    def tok_local(i):
        return pltpu.make_async_copy(
            tok_hbm.at[:, pl.ds((i * 2 + c) * 256, 256)],
            tok.at[pl.ds(0, ROWS), pl.ds(i * 256, 256)], tl_sem.at[0])

    def tok_remote(i):
        return remote(
            tok_hbm.at[:, pl.ds((i * 2 + 1 - c) * 256, 256)],
            tok.at[pl.ds(ROWS, ROWS), pl.ds(i * 256, 256)], ts_sem.at[0], tr_sem.at[0], sibling)

    barrier = pltpu.get_barrier_semaphore()

    for o in (1, 2, 3):
        across = (up(z, o) * 8 + y * 2 + (1 - c), x)
        for partner in (along_x(o), along_y(o), along_z(o), across):
            pl.semaphore_signal(barrier, inc=1, device_id=partner, device_id_type=MESH)
    pl.semaphore_signal(barrier, inc=1, device_id=sibling, device_id_type=MESH)
    own_k.start()
    own_w.start()

    def heads_in(h, carry):
        q_in(h).start()
        do_in(h).start()
        return carry

    lax.fori_loop(0, HEADS, heads_in, 0)

    cut = jnp.sum(jnp.where(doc_ref[0:1, :] == 0, 1, 0), axis=1, keepdims=True)
    k_pos = lax.broadcasted_iota(jnp.int32, (KEYS, ROWS), 0)
    q_pos = lax.broadcasted_iota(jnp.int32, (KEYS, ROWS), 1) + x * ROWS
    allowed = (k_pos <= q_pos) & ((k_pos < cut) == (q_pos < cut))
    bias[...] = jnp.where(allowed, 0.0, -1e30)

    blk = lax.broadcasted_iota(jnp.int32, (8, ROWS), 1) // BLK
    dest = jnp.zeros((8, ROWS), jnp.int32)
    for b in range(32):
        dest = jnp.where(blk == b, dest_ref[b], dest)
    dest_dp, target = dest // 128, dest % 32
    rank = jnp.zeros((8, ROWS), jnp.int32)
    for b in range(31):
        rank = rank + jnp.where((blk > b) & (dest_dp == dest_ref[b] // 128), 1, 0)
    pos = (dest_dp * 2 + rank)[0:1, :]
    r_i = lax.broadcasted_iota(jnp.int32, (SLOTS, ROWS), 0)
    c_i = lax.broadcasted_iota(jnp.int32, (SLOTS, ROWS), 1)
    same_row = (r_i % BLK) == (c_i % BLK)
    fwd[...] = jnp.where(same_row & ((r_i // BLK) == pos), 1.0, 0.0).astype(BF)
    lab_rows = jnp.broadcast_to((target + 1).astype(F32)[0:1, :], (HEAD, ROWS))
    lsnd[...] = nn(fwd[...], jnp.transpose(lab_rows).astype(BF)).astype(BF)
    pl.semaphore_wait(barrier, 13)
    for o in (1, 2, 3):
        pl.semaphore_signal(relay, inc=1, device_id=along_y(o), device_id_type=MESH)

    def w_x(o):
        return remote(w_hbm, wh.at[z, y, pl.ds(x * 64, 64)], wx_s.at[0], wx_r.at[0], along_x(o))

    def k_x(o, e):
        cols = pl.ds(e * HEAD, HEAD)
        return remote(k_hbm.at[:, cols], kf.at[pl.ds(x * ROWS, ROWS), cols], k_s.at[0], k_r.at[e], along_x(o))

    for o in (1, 3, 2):
        k_x(o, 0).start()
        w_x(o).start()

    def peers(send_buf, recv_buf, ss, rs):
        def one(o):
            p = (me + o) % 32
            return remote(send_buf.at[pl.ds(p * 16, 16)], recv_buf.at[pl.ds(me * 16, 16)], ss.at[0], rs.at[0], (p, x))

        def start():
            def body(o, carry):
                one(o).start()
                return carry

            lax.fori_loop(1, 32, body, 0)
            mine = pl.ds(pl.multiple_of(me * 16, 16), 16)
            recv_buf[mine, :] = send_buf[mine, :]

        def wait_recv():
            landed(recv_buf.at[pl.ds(0, 496)], rs.at[0])

        def wait_send():
            landed(send_buf.at[pl.ds(0, 496)], ss.at[0])

        return start, wait_recv, wait_send

    l_start, l_recv, l_done = peers(lsnd, lrcv, l_s, l_r)
    a_start, a_recv, a_done = peers(snd, rcv, a_s, a_r)
    b_start, b_recv, b_done = peers(bsnd, brcv, b_s, b_r)

    def start_tokens(i, carry):
        tok_local(i).start()
        tok_remote(i).start()
        return carry


    def w_2a(o):
        blk = wh.at[z, y, pl.ds(0, 128)]
        return remote(blk, blk, w2_s.at[0], w2_r.at[o], along_y(o))

    def w_2b(o):
        blk = wh.at[z, y, pl.ds(128, 128)]
        return remote(blk, blk, w2_s.at[0], w2_r.at[4 + o], along_z(o))

    def w_3a(j, m):
        yy = up(y, j)
        if m < 2:
            blk = wh.at[z, yy, pl.ds(0, 128)]
        elif m == 2:
            blk = wh.at[up(z, 3), yy, pl.ds(0, 64)]
        else:
            blk = wh.at[up(z, 1), yy, pl.ds(64, 64)]
        i = j * 2 + m if m < 2 else 16
        return remote(blk, blk, w3_s.at[0], w3_r.at[i], along_z(1 if m % 2 == 0 else 3))

    def w_3b(j, m):
        zz = up(z, j)
        if m < 2:
            blk = wh.at[zz, y, pl.ds(128, 128)]
        elif m == 2:
            blk = wh.at[zz, up(y, 3), pl.ds(128, 64)]
        else:
            blk = wh.at[zz, up(y, 1), pl.ds(192, 64)]
        i = 8 + j * 2 + m if m < 2 else 16
        return remote(blk, blk, w3_s.at[0], w3_r.at[i], along_y(1 if m % 2 == 0 else 3))

    def w_begin():
        own_w.wait()
        landed(wh.at[0, 0, pl.ds(0, 192)], wx_r.at[0])
        for o in (1, 3, 2):
            w_2a(o).start()
            w_2b(o).start()
        for m in (0, 1):
            w_3a(0, m).start()
            w_3b(0, m).start()

    def w_full(j):
        w_2a((4 - j) % 4).wait_recv()
        w_2b((4 - j) % 4).wait_recv()
        for m in (0, 1):
            w_3a(j, m).start()
            w_3b(j, m).start()

    def w_forward(j):
        for m in (0, 1):
            w_3a(j, m).wait_recv()
            w_3a(j, m + 2).start()
            w_3b(j, m).wait_recv()
            w_3b(j, m + 2).start()

    def w_end():
        landed(wh.at[0], w3_r.at[16])
        landed(wh.at[0, 0, pl.ds(0, 192)], wx_s.at[0])
        landed(wh.at[0, pl.ds(0, 3)], w2_s.at[0])
        landed(wh.at[pl.ds(0, 3)], w3_s.at[0])

    def sum_x(ss, rs):
        def one(o, e):
            cols = pl.ds(e * HEAD, HEAD)
            return remote(gsend.at[pl.ds(up(x, o) * ROWS, ROWS), cols], gin.at[o - 1, :, cols], ss.at[0], rs.at[0], along_x(o))

        def start(e):
            cols = pl.ds(e * HEAD, HEAD)
            gsend[:, cols] = acc[:, cols].astype(BF)
            for o in (1, 3, 2):
                one(o, e).start()

        def finish():
            landed(gin, rs.at[0])
            own = acc[pl.ds(pl.multiple_of(x * ROWS, ROWS), ROWS), :]
            total = own + gin[0].astype(F32) + gin[1].astype(F32) + gin[2].astype(F32)
            landed(gin, ss.at[0])
            return total

        return start, finish

    dv_start, dv_finish = sum_x(dv_s, dv_r)
    dk_start, dk_finish = sum_x(dk_s, dk_r)

    def at_head(h, where, act):
        pl.when(h == where)(act)

    own_k.wait()

    def three(e):
        return kf.at[pl.ds(0, 768), pl.ds(e * HEAD, HEAD)]

    def k_send(e):
        for o in (1, 3, 2):
            k_x(o, e).start()

    def w_rest():
        for j in (1, 3, 2):
            w_full(j)
        w_forward(0)

    w_begin()
    k_send(1)
    k_send(2)
    pl.semaphore_wait(relay, 3)
    l_start()
    lax.fori_loop(0, 16, start_tokens, 0)

    def first(e, carry):
        for i in range(KV_HEADS):
            @pl.when(e == i)
            def _():
                landed(three(i), k_r.at[i])
                if i == 1:
                    k_send(3)
        at_head(e, 2, w_rest)
        at_head(e, 3, lambda: w_forward(1))
        landed(qs.at[e], q_sem.at[e])
        landed(dos.at[e], do_sem.at[e])
        ecol = pl.ds(pl.multiple_of(e * HEAD, HEAD), HEAD)
        keys = kf[:, ecol]
        for hh in range(8):
            rows = slice(hh * ROWS, (hh + 1) * ROWS)
            s = nt(keys, qs[e, rows, :]) * (SCALE * LOG2E) + bias[...]
            m = jnp.max(s, axis=0, keepdims=True)
            p = jnp.exp2(s - m)
            inv = 1.0 / jnp.sum(p, axis=0, keepdims=True)
            prob[e, :, rows] = p.astype(BF)
            inv_row[e * 8 + hh] = inv
            inv_rows = jnp.transpose(jnp.broadcast_to(inv, (HEAD, ROWS)))
            dos[e, rows, :] = (dos[e, rows, :].astype(F32) * inv_rows).astype(BF)
        acc[:, ecol] = nn(prob[e], dos[e])
        for i in range(KV_HEADS):
            at_head(e, i, lambda i=i: dv_start(i))
        return carry

    lax.fori_loop(0, KV_HEADS, first, 0)
    w_forward(3)
    l_recv()
    lab = lrcv[...].astype(F32)
    want = (c_i // BLK + 1).astype(F32)
    bwd_t[...] = jnp.where(same_row & (jnp.concatenate([lab, lab], axis=1) == want), 1.0, 0.0).astype(BF)
    w_forward(2)

    bsnd[...] = nn(bwd_t[...], dv_finish().astype(BF)).astype(BF)
    b_start()

    landed(tok.at[pl.ds(0, ROWS)], tl_sem.at[0])
    landed(tok.at[pl.ds(ROWS, ROWS)], tr_sem.at[0])
    w_end()

    def project(first_row):
        total = None
        for zz in range(4):
            term = nn(tok[pl.ds(first_row, ROWS), pl.ds(zz * 1024, 1024)], wh[zz].reshape(1024, FEAT))
            total = term if total is None else total + term
        return total

    give_part = remote(part, part_in, p_s.at[0], p_r.at[0], sibling)
    part[...] = project(ROWS)
    give_part.start()
    mine = project(0)
    give_part.wait_recv()
    values = (mine + part_in[...]).astype(BF)
    snd[...] = nn(fwd[...], values).astype(BF)
    a_start()

    b_recv()
    dvl[pl.ds(0, ROWS), :] = tn(fwd[...], brcv[...]).astype(BF)
    give_dvl = remote(dvl.at[pl.ds(0, ROWS)], dvl.at[pl.ds(ROWS, ROWS)], d_s.at[0], d_r.at[0], sibling)
    give_dvl.start()
    give_dvl.wait_recv()

    def weight_blocks(i, carry):
        for n in range(8):
            cols = pl.ds(pl.multiple_of(i * 2048 + n * 256, 256), 256)
            wh[i * 2 + n // 4, n % 4] = tn(tok[:, cols], dvl[...]).astype(BF)
        return carry

    lax.fori_loop(0, 2, weight_blocks, 0)

    a_rows, b_rows = pl.ds(0, 128), pl.ds(128, 128)
    low2, high2 = pl.ds(0, 2), pl.ds(2, 2)

    g_1 = [
        remote(wh.at[up(z, 2), low2, a_rows], f1a, g_s.at[0], g_r.at[0], along_z(1)),
        remote(wh.at[up(z, 2), high2, a_rows], f2a, g_s.at[0], g_r.at[1], along_z(3)),
        remote(wh.at[low2, up(y, 2), b_rows], f1b, g_s.at[0], g_r.at[2], along_y(1)),
        remote(wh.at[high2, up(y, 2), b_rows], f2b, g_s.at[0], g_r.at[3], along_y(3)),
        remote(wh.at[up(z, 1), high2, a_rows], mpa.at[high2], g_s.at[0], g_r.at[4], along_z(1)),
        remote(wh.at[up(z, 3), low2, a_rows], mma.at[low2], g_s.at[0], g_r.at[5], along_z(3)),
        remote(wh.at[high2, up(y, 1), b_rows], mpb.at[high2], g_s.at[0], g_r.at[6], along_y(1)),
        remote(wh.at[low2, up(y, 3), b_rows], mmb.at[low2], g_s.at[0], g_r.at[7], along_y(3)),
    ]
    g_2 = [
        remote(wh.at[up(z, 1), low2, a_rows], mpa.at[low2], g_s.at[0], g_r.at[4], along_z(1)),
        remote(wh.at[up(z, 3), high2, a_rows], mma.at[high2], g_s.at[0], g_r.at[5], along_z(3)),
        remote(wh.at[low2, up(y, 1), b_rows], mpb.at[low2], g_s.at[0], g_r.at[6], along_y(1)),
        remote(wh.at[high2, up(y, 3), b_rows], mmb.at[high2], g_s.at[0], g_r.at[7], along_y(3)),
    ]

    def g_3a(o):
        return remote(wh.at[z, up(y, o), a_rows], s2a.at[o - 1], g2_s.at[0], g2_r.at[0], along_y(o))

    def g_3b(o):
        return remote(wh.at[up(z, o), y, b_rows], s2b.at[o - 1], g2_s.at[0], g2_r.at[1], along_z(o))

    def g_x(o):
        rows = pl.ds(up(x, o) * 64, 64)
        return remote(wh.at[z, y, rows], s3.at[o - 1], g3_s.at[0], g3_r.at[0], along_x(o))

    def bsum(*terms):
        total = terms[0].astype(F32)
        for t in terms[1:]:
            total = total + t.astype(F32)
        return total

    def g_step1():
        for i in range(4):
            g_1[i].wait_recv()
            if i == 0:
                wh[up(z, 1), 0:2, 0:128] = bsum(wh[up(z, 1), 0:2, 0:128], f1a[...]).astype(BF)
            elif i == 1:
                wh[up(z, 3), 2:4, 0:128] = bsum(wh[up(z, 3), 2:4, 0:128], f2a[...]).astype(BF)
            elif i == 2:
                wh[0:2, up(y, 1), 128:256] = bsum(wh[0:2, up(y, 1), 128:256], f1b[...]).astype(BF)
            else:
                wh[2:4, up(y, 3), 128:256] = bsum(wh[2:4, up(y, 3), 128:256], f2b[...]).astype(BF)
            g_2[i].start()

    def g_step2():
        for i, buf in enumerate((mpa, mma, mpb, mmb)):
            landed(buf, g_r.at[4 + i])
        for i in range(4):
            wh[z, i, 0:128] = bsum(wh[z, i, 0:128], mpa[i], mma[i]).astype(BF)
            wh[i, y, 128:256] = bsum(wh[i, y, 128:256], mpb[i], mmb[i]).astype(BF)
        for o in (1, 3, 2):
            g_3a(o).start()
            g_3b(o).start()

    def g_step3():
        landed(s2a, g2_r.at[0])
        landed(s2b, g2_r.at[1])
        wh[z, y, 0:128] = bsum(wh[z, y, 0:128], s2a[0], s2a[1], s2a[2]).astype(BF)
        wh[z, y, 128:256] = bsum(wh[z, y, 128:256], s2b[0], s2b[1], s2b[2]).astype(BF)
        for o in (1, 3, 2):
            g_x(o).start()

    def g_step4():
        landed(s3, g3_r.at[0])
        rows = pl.ds(pl.multiple_of(x * 64, 64), 64)
        wg_ref[...] = bsum(wh[z, y, rows, :], s3[0], s3[1], s3[2])
        landed(wh.at[pl.ds(0, 3)], g_s.at[0])
        landed(wh.at[0, pl.ds(0, 3)], g2_s.at[0])
        landed(s3, g3_s.at[0])

    for d in g_1[:4]:
        d.start()

    a_recv()
    mine_rows = pl.ds(pl.multiple_of(x * ROWS, ROWS), ROWS)
    vf[mine_rows, :] = tn(bwd_t[...], rcv[...]).astype(BF)

    def v_x(o, e):
        blk = vf.at[pl.ds(x * ROWS, ROWS), pl.ds(e * HEAD, HEAD)]
        return remote(blk, blk, v_s.at[0], v_r.at[e], along_x(o))

    def v_send(e):
        for o in (1, 3, 2):
            v_x(o, e).start()

    v_send(0)
    for d in g_1[4:]:
        d.start()
    v_send(1)
    g_step1()
    for e in range(KV_HEADS):
        kt[e] = jnp.transpose(kf[:, pl.ds(e * HEAD, HEAD)].astype(F32)).astype(BF)

    def dq_out(h):
        return pltpu.make_async_copy(
            qs.at[h // 8, pl.ds((h % 8) * ROWS, ROWS)], dq_hbm.at[:, pl.ds(h * HEAD, HEAD)], dq_s.at[0])

    def second(e, carry):
        for i in range(KV_HEADS):
            @pl.when(e == i)
            def _():
                landed(three(i), v_r.at[i])
                if i < 2:
                    v_send(i + 2)
        at_head(e, 2, g_step2)
        ecol = pl.ds(pl.multiple_of(e * HEAD, HEAD), HEAD)
        values_e = vf[:, ecol]
        for hh in range(8):
            rows = slice(hh * ROWS, (hh + 1) * ROWS)
            dp = nt(values_e, dos[e, rows, :])
            p = prob[e, :, rows].astype(F32)
            rd = jnp.sum(p * dp, axis=0, keepdims=True) * inv_row[e * 8 + hh]
            prob[e, :, rows] = (p * (dp - rd)).astype(BF)
        acc[:, ecol] = nn(prob[e], qs[e])
        dq_t = nn(kt[e], prob[e]) * SCALE
        for hh in range(8):
            rows = slice(hh * ROWS, (hh + 1) * ROWS)
            qs[e, rows, :] = jnp.transpose(dq_t[:, rows]).astype(BF)
        for hh in range(8):
            dq_out(e * 8 + hh).start()
        for i in range(KV_HEADS):
            at_head(e, i, lambda i=i: dk_start(i))
        return carry

    lax.fori_loop(0, KV_HEADS, second, 0)

    g_step3()
    dk_ref[...] = (dk_finish() * SCALE).astype(BF)
    g_step4()

    landed(qs, dq_s.at[0])
    landed(kf.at[pl.ds(0, 768)], k_s.at[0])
    landed(vf.at[pl.ds(0, 768)], v_s.at[0])
    l_done()
    a_done()
    b_done()
    give_part.wait_send()
    give_dvl.wait_send()

    landed(tok.at[pl.ds(ROWS, ROWS)], ts_sem.at[0])


def per_device(tokens, w, queries, keys, cotangent, block_dest, doc_ids):
    vm = lambda shape, t: pltpu.VMEM(shape, t)
    dma = lambda n: pltpu.SemaphoreType.DMA((n,))
    anyspec = pl.BlockSpec(memory_space=pl.ANY)
    vspec = pl.BlockSpec(memory_space=pltpu.VMEM)
    scratch = [
        vm((512, 4096), BF),
        vm((4, 4, 256, FEAT), BF),
        vm((KV_HEADS, 8 * ROWS, HEAD), BF),
        vm((KV_HEADS, 8 * ROWS, HEAD), BF),
        vm((KEYS, FEAT), BF),
        vm((KV_HEADS, HEAD, KEYS), BF),
        vm((KEYS, FEAT), BF),
        vm((KV_HEADS, KEYS, 8 * ROWS), BF),
        vm((HEADS, 1, ROWS), F32),
        vm((KEYS, ROWS), F32),
        vm((KEYS, FEAT), F32),
        vm((ROWS, FEAT), F32),
        vm((ROWS, FEAT), F32),
        vm((SLOTS, FEAT), BF),
        vm((SLOTS, FEAT), BF),
        vm((SLOTS, 128), BF),
        vm((SLOTS, 128), BF),
        vm((SLOTS, ROWS), BF),
        vm((SLOTS, ROWS), BF),
        vm((SLOTS, FEAT), BF),
        vm((SLOTS, FEAT), BF),
        vm((512, FEAT), BF),
        vm((KEYS, FEAT), BF),
        vm((3, ROWS, FEAT), BF),
        vm((2, 128, FEAT), BF),
        vm((2, 128, FEAT), BF),
        vm((2, 128, FEAT), BF),
        vm((2, 128, FEAT), BF),
        vm((4, 128, FEAT), BF),
        vm((4, 128, FEAT), BF),
        vm((4, 128, FEAT), BF),
        vm((4, 128, FEAT), BF),
        vm((3, 128, FEAT), BF),
        vm((3, 128, FEAT), BF),
        vm((3, 64, FEAT), BF),
        dma(2), dma(4), dma(4), dma(1), dma(1), dma(1),
        dma(1), dma(1), dma(1), dma(8), dma(1), dma(17), dma(1), dma(4),
        dma(1), dma(1), dma(1), dma(1), dma(1), dma(1),
        dma(1), dma(1), dma(1), dma(1),
        dma(1), dma(4), dma(1), dma(1), dma(1), dma(1),
        dma(1), dma(8), dma(1), dma(2), dma(1), dma(1), dma(1),
        pltpu.SemaphoreType.REGULAR,
    ]
    return pl.pallas_call(
        kernel,
        out_shape=(
            jax.ShapeDtypeStruct((ROWS, 4096), BF),
            jax.ShapeDtypeStruct((ROWS, FEAT), BF),
            jax.ShapeDtypeStruct((64, FEAT), F32),
        ),
        in_specs=[anyspec] * 5 + [pl.BlockSpec(memory_space=pltpu.SMEM), vspec],
        out_specs=(anyspec, vspec, vspec),
        scratch_shapes=scratch,
        compiler_params=pltpu.CompilerParams(
            collective_id=0, has_side_effects=True, vmem_limit_bytes=62 * 1024 * 1024
        ),
        name="attention_and_weights",
    )(tokens, w, queries, keys, cotangent, block_dest, doc_ids)


def solution(mesh):
    both = P(("dp", "sp"), None)
    return jax.shard_map(
        per_device,
        mesh=mesh,
        in_specs=(both, both, both, both, both, P(("dp", "sp")), P("dp", None)),
        out_specs=(both, both, both),
        check_vma=False,
    )
```

time: 159 us -> 97.6 us (0.61)
  Pallas kernels: 149 us -> 92.2 us
  local copies, waits for them, and re-layouts: 7.52 us -> 4.54 us
    pallas_call x1, Pallas kernels: 149 us -> 92.2 us  [per_device(): pl.pallas_call(kernel, out_shape=(jax.ShapeDtypeStruct((ROWS, 4096), BF),...]
    broadcast_in_dim x6 -> x0, local copies, waits for them, and re-layouts: 2.88 us -> none  [the longest x1 1.3 us: per_device(): doc = jnp.broadcast_to(doc_ids, (8, KEYS))]
where the time goes in v2:
time: 97.6 us; the launch traced here: 97.4 us
  Pallas kernels  92.2 us (94%)
  local copies, waits for them, and re-layouts  4.54 us (5%)
    pallas_call x1, Pallas kernels, per_device(): pl.pallas_call(kernel, out_shape=(jax.ShapeDtypeStruct((ROWS, 4096), BF),...  92.2 us
    unnamed x7, local copies, waits for them, and re-layouts  4.54 us

profile of v2, /device:TPU:0, one launch (start us, length us, event | category | flops | bytes accessed | tf_op | source)
XLA Modules:
  0.0 97.4 jit_solution(2149097099280934529)
XLA Ops:
  0.6 92.2 %attention_and_weights.1 = (bf16[256,4096]{1,0:T(8,128)(2,1)}, bf16[256,512]{1,0:T(8,128)(2,1)}, f32[64,512]{1,0:T(8,128)}) custom-call(bf16[256,8192]{1,0:T(8,128)(2,1)} %tok_hbm.1, bf16[64,512]{1,0:T(8,128)(2,1)} %w_hbm.1, bf16[256,4096]{1,0:T(8,128)(2,1)} %q_hbm.1, bf16[256,512]{1,0:T(8,128)(2,1)} %k_hbm.1, bf16[256,4096]{1,0:T(8,128)(2,1)} %do_hbm.1, ...), custom_call_target="tpu_custom_call" | custom-call | tf_op jit(solution)/shard_map/attention_and_weights/pallas_call | solution.py:559
  92.8 0.0 copy-start
  92.8 0.0 copy-start.1
  92.8 3.2 %copy.13 = bf16[256,4096]{1,0:T(8,128)(2,1)} copy(bf16[256,4096]{1,0:T(8,128)(2,1)} %get-tuple-element.6) | data formatting | bytes 4194304
  96.0 0.0 copy-done
  96.0 0.7 copy.14
  96.7 0.0 copy-done.1
  96.7 0.7 copy.15
Async XLA Ops:
  92.8 3.2 %copy-start = (bf16[256,512]{1,0:T(8,128)(2,1)S(1)}, bf16[256,512]{1,0:T(8,128)(2,1)}, u32[]{:S(2)}) copy-start(bf16[256,512]{1,0:T(8,128)(2,1)} %get-tuple-element.7) | copy-start | bytes 786436
  92.8 3.9 %copy-start.1 = (f32[64,512]{1,0:T(8,128)S(1)}, f32[64,512]{1,0:T(8,128)}, u32[]{:S(2)}) copy-start(f32[64,512]{1,0:T(8,128)} %get-tuple-element.8) | copy-start | bytes 393220

commit v3 on v2

--- a/solution.py
+++ b/solution.py
@@ -145,8 +145,9 @@
         return remote(k_hbm.at[:, cols], kf.at[pl.ds(x * ROWS, ROWS), cols], k_s.at[0], k_r.at[e], along_x(o))
 
     for o in (1, 3, 2):
+        w_x(o).start()
+    for o in (1, 3, 2):
         k_x(o, 0).start()
-        w_x(o).start()
 
     def peers(send_buf, recv_buf, ss, rs):
         def one(o):
@@ -328,19 +329,26 @@
 
     landed(tok.at[pl.ds(0, ROWS)], tl_sem.at[0])
     landed(tok.at[pl.ds(ROWS, ROWS)], tr_sem.at[0])
-    w_end()
-
-    def project(first_row):
+
+    def project(rows, blocks):
         total = None
-        for zz in range(4):
-            term = nn(tok[pl.ds(first_row, ROWS), pl.ds(zz * 1024, 1024)], wh[zz].reshape(1024, FEAT))
+        for dz, dy in blocks:
+            zz, yy = up(z, dz), up(y, dy)
+            cols = pl.ds(pl.multiple_of((zz * 4 + yy) * 256, 256), 256)
+            term = nn(tok[rows, cols], wh[zz, yy])
             total = term if total is None else total + term
         return total
 
-    give_part = remote(part, part_in, p_s.at[0], p_r.at[0], sibling)
-    part[...] = project(ROWS)
+    near = [(dz, dy) for dz in (0, 1, 3) for dy in (0, 1, 3)]
+    far = [(2, dy) for dy in range(4)] + [(dz, 2) for dz in (0, 1, 3)]
+    part[...] = project(pl.ds(0, 512), near)
+    w_end()
+
+
+    give_part = remote(part.at[pl.ds(ROWS, ROWS)], part_in, p_s.at[0], p_r.at[0], sibling)
+    part[pl.ds(ROWS, ROWS), :] += project(pl.ds(ROWS, ROWS), far)
     give_part.start()
-    mine = project(0)
+    mine = part[pl.ds(0, ROWS), :] + project(pl.ds(0, ROWS), far)
     give_part.wait_recv()
     values = (mine + part_in[...]).astype(BF)
     snd[...] = nn(fwd[...], values).astype(BF)
@@ -454,7 +462,6 @@
     for d in g_1[4:]:
         d.start()
     v_send(1)
-    g_step1()
     for e in range(KV_HEADS):
         kt[e] = jnp.transpose(kf[:, pl.ds(e * HEAD, HEAD)].astype(F32)).astype(BF)
 
@@ -469,7 +476,8 @@
                 landed(three(i), v_r.at[i])
                 if i < 2:
                     v_send(i + 2)
-        at_head(e, 2, g_step2)
+        at_head(e, 1, g_step1)
+        at_head(e, 3, g_step2)
         ecol = pl.ds(pl.multiple_of(e * HEAD, HEAD), HEAD)
         values_e = vf[:, ecol]
         for hh in range(8):
@@ -507,6 +515,22 @@
     landed(tok.at[pl.ds(ROWS, ROWS)], ts_sem.at[0])
 
 
+def hand_on(dq_in, dk_in, wg_in, dq_out, dk_out, wg_out, dq_v, dk_v, wg_v, sem):
+    steps = [(dk_in, dk_v, dk_out), (wg_in, wg_v, wg_out)]
+    for i in range(8):
+        rows = pl.ds(i * 32, 32)
+        steps.append((dq_in.at[rows], dq_v.at[rows], dq_out.at[rows]))
+    into = [pltpu.make_async_copy(a, v, sem.at[0, i]) for i, (a, v, _) in enumerate(steps)]
+    away = [pltpu.make_async_copy(v, b, sem.at[1, i]) for i, (_, v, b) in enumerate(steps)]
+    for copy in into:
+        copy.start()
+    for i, copy in enumerate(into):
+        copy.wait()
+        away[i].start()
+    for copy in away:
+        copy.wait()
+
+
 def per_device(tokens, w, queries, keys, cotangent, block_dest, doc_ids):
     vm = lambda shape, t: pltpu.VMEM(shape, t)
     dma = lambda n: pltpu.SemaphoreType.DMA((n,))
@@ -524,7 +548,7 @@
         vm((HEADS, 1, ROWS), F32),
         vm((KEYS, ROWS), F32),
         vm((KEYS, FEAT), F32),
-        vm((ROWS, FEAT), F32),
+        vm((2 * ROWS, FEAT), F32),
         vm((ROWS, FEAT), F32),
         vm((SLOTS, FEAT), BF),
         vm((SLOTS, FEAT), BF),
@@ -556,7 +580,7 @@
         dma(1), dma(8), dma(1), dma(2), dma(1), dma(1), dma(1),
         pltpu.SemaphoreType.REGULAR,
     ]
-    return pl.pallas_call(
+    raw = pl.pallas_call(
         kernel,
         out_shape=(
             jax.ShapeDtypeStruct((ROWS, 4096), BF),
@@ -571,6 +595,15 @@
         ),
         name="attention_and_weights",
     )(tokens, w, queries, keys, cotangent, block_dest, doc_ids)
+    return pl.pallas_call(
+        hand_on,
+        out_shape=tuple(jax.ShapeDtypeStruct(r.shape, r.dtype) for r in raw),
+        in_specs=[anyspec] * 3,
+        out_specs=(anyspec,) * 3,
+        scratch_shapes=[
+            vm((ROWS, 4096), BF), vm((ROWS, FEAT), BF), vm((64, FEAT), F32), pltpu.SemaphoreType.DMA((2, 10))],
+        name="hand_on",
+    )(*raw)
 
 
 def solution(mesh):

time: 97.6 us -> 92.6 us (0.949)
  local copies, waits for them, and re-layouts: 4.54 us -> 0 us
    unnamed x7 -> x0, local copies, waits for them, and re-layouts: 4.54 us -> none
    pallas_call x1, Pallas kernels: 92.2 us -> 89 us  [per_device(): pl.pallas_call(kernel, out_shape=(jax.ShapeDtypeStruct((ROWS, 4096), BF),...]
    pallas_call x0 -> x1, Pallas kernels: none -> 2.57 us  [per_device(): pl.pallas_call(hand_on, out_shape=tuple((jax.ShapeDtypeStruct(r.shape, r....]
where the time goes in v3:
time: 92.6 us; the launch traced here: 92.4 us
  Pallas kernels  91.6 us (99%)
    pallas_call x1, Pallas kernels, per_device(): pl.pallas_call(kernel, out_shape=(jax.ShapeDtypeStruct((ROWS, 4096), BF),...  89 us
    pallas_call x1, Pallas kernels, per_device(): pl.pallas_call(hand_on, out_shape=tuple((jax.ShapeDtypeStruct(r.shape, r....  2.57 us

profile of v3, /device:TPU:0, one launch (start us, length us, event | category | flops | bytes accessed | tf_op | source)
XLA Modules:
  0.0 92.4 jit_solution(11685286275634985170)
XLA Ops:
  0.6 89.0 %attention_and_weights.1 = (bf16[256,4096]{1,0:T(8,128)(2,1)}, bf16[256,512]{1,0:T(8,128)(2,1)}, f32[64,512]{1,0:T(8,128)}) custom-call(bf16[256,8192]{1,0:T(8,128)(2,1)} %tok_hbm.1, bf16[64,512]{1,0:T(8,128)(2,1)} %w_hbm.1, bf16[256,4096]{1,0:T(8,128)(2,1)} %q_hbm.1, bf16[256,512]{1,0:T(8,128)(2,1)} %k_hbm.1, bf16[256,4096]{1,0:T(8,128)(2,1)} %do_hbm.1, ...), custom_call_target="tpu_custom_call" | custom-call | tf_op jit(solution)/shard_map/attention_and_weights/pallas_call | solution.py:583
  89.7 2.6 %hand_on.1 = (bf16[256,4096]{1,0:T(8,128)(2,1)}, bf16[256,512]{1,0:T(8,128)(2,1)}, f32[64,512]{1,0:T(8,128)}) custom-call(bf16[256,4096]{1,0:T(8,128)(2,1)} %get-tuple-element.6.dq_in, bf16[256,512]{1,0:T(8,128)(2,1)} %get-tuple-element.7.dk_in, f32[64,512]{1,0:T(8,128)} %get-tuple-element.8.wg_in), custom_call_target="tpu_custom_call" | custom-call | tf_op jit(solution)/shard_map/hand_on/pallas_call | solution.py:598

commit v4 on v3

--- a/solution.py
+++ b/solution.py
@@ -295,7 +295,12 @@
                 landed(three(i), k_r.at[i])
                 if i == 1:
                     k_send(3)
-        at_head(e, 2, w_rest)
+        at_head(e, 1, lambda: w_full(1))
+        @pl.when(e == 2)
+        def _():
+            w_full(3)
+            w_full(2)
+            w_forward(0)
         at_head(e, 3, lambda: w_forward(1))
         landed(qs.at[e], q_sem.at[e])
         landed(dos.at[e], do_sem.at[e])

time: 92.6 us -> 90.4 us (0.976)
  Pallas kernels: 91.6 us -> 89.4 us
    pallas_call x1, Pallas kernels: 89 us -> 86.9 us  [per_device(): pl.pallas_call(kernel, out_shape=(jax.ShapeDtypeStruct((ROWS, 4096), BF),...]
where the time goes in v4:
time: 90.4 us; the launch traced here: 90.2 us
  Pallas kernels  89.4 us (99%)
    pallas_call x1, Pallas kernels, per_device(): pl.pallas_call(kernel, out_shape=(jax.ShapeDtypeStruct((ROWS, 4096), BF),...  86.9 us
    pallas_call x1, Pallas kernels, per_device(): pl.pallas_call(hand_on, out_shape=tuple((jax.ShapeDtypeStruct(r.shape, r....  2.57 us

profile of v4, /device:TPU:0, one launch (start us, length us, event | category | flops | bytes accessed | tf_op | source)
XLA Modules:
  0.0 90.2 jit_solution(4597759788756218473)
XLA Ops:
  0.6 86.9 %attention_and_weights.1 = (bf16[256,4096]{1,0:T(8,128)(2,1)}, bf16[256,512]{1,0:T(8,128)(2,1)}, f32[64,512]{1,0:T(8,128)}) custom-call(bf16[256,8192]{1,0:T(8,128)(2,1)} %tok_hbm.1, bf16[64,512]{1,0:T(8,128)(2,1)} %w_hbm.1, bf16[256,4096]{1,0:T(8,128)(2,1)} %q_hbm.1, bf16[256,512]{1,0:T(8,128)(2,1)} %k_hbm.1, bf16[256,4096]{1,0:T(8,128)(2,1)} %do_hbm.1, ...), custom_call_target="tpu_custom_call" | custom-call | tf_op jit(solution)/shard_map/attention_and_weights/pallas_call | solution.py:588
  87.5 2.6 %hand_on.1 = (bf16[256,4096]{1,0:T(8,128)(2,1)}, bf16[256,512]{1,0:T(8,128)(2,1)}, f32[64,512]{1,0:T(8,128)}) custom-call(bf16[256,4096]{1,0:T(8,128)(2,1)} %get-tuple-element.6.dq_in, bf16[256,512]{1,0:T(8,128)(2,1)} %get-tuple-element.7.dk_in, f32[64,512]{1,0:T(8,128)} %get-tuple-element.8.wg_in), custom_call_target="tpu_custom_call" | custom-call | tf_op jit(solution)/shard_map/hand_on/pallas_call | solution.py:603
